TPU v7x, 32 devices: a whole 2x2x4 slice. The times are simulated.
32 devices in a mesh: row: 4 (over x, core), pair: 8 (over z, y).
Axes of the slice: x: 2, y: 2, z: 4, core: 2. Of those that a mesh axis runs over, the one named last changes fastest.
Arguments:
- weight: float32 [14336, 2048], P('row', 'pair'), may hold values from -300 to 300
- move_flags: int32 [2, 8], P(None, 'pair'), may hold values from 0 to 1
Outputs:
- columns: float32 [14336, 2048], P('row', 'pair')
- norm_ratios: float32 [2048], P('pair')
All inputs are finite; a program needn't handle non-finite values.
Results may differ from a plain program's by a relative error of at most 0.0003.
Values sent between devices are 32-bit elements; how exact they have to be, the bound alone decides.
A program may use at most 64 MiB of HBM per device.

v0:
```python
import functools

import jax
import jax.numpy as jnp
from jax import lax
from jax.experimental import pallas as pl
from jax.experimental.pallas import tpu as pltpu
from jax.sharding import PartitionSpec as P

SWEEPS = 2
POLAR = 8
ROUNDS = 3

MESH = pl.DeviceIdType.MESH
precise = lax.Precision.HIGH


def from_behind(block, axis, distance):
    devices = range(lax.axis_size(axis))
    route = [((i - distance) % len(devices), i) for i in devices]
    return lax.ppermute(block, axis, route)


def contract(left, right):
    return lax.dot_general(
        left, right, (((0,), (0,)), ((), ())), precision=precise, preferred_element_type=jnp.float32
    )


def times(left, right):
    return jnp.dot(left, right, precision=precise, preferred_element_type=jnp.float32)


def halves(value):
    high = value.astype(jnp.bfloat16)
    low = (value - high.astype(jnp.float32)).astype(jnp.bfloat16)
    return high, low


def product3(left, right):
    return jnp.dot(
        jnp.concatenate([left[0], left[0], left[1]], axis=1),
        jnp.concatenate([right[0], right[1], right[0]], axis=0),
        preferred_element_type=jnp.float32,
    )


def iterate(gram):
    gram_parts = halves(gram)
    product = gram
    for sweep in range(SWEEPS):
        if sweep:
            product = product3(gram_parts, halves(product))
        parts = halves(product)
        normal = product3(parts, parts)
        scaled = product / jnp.sqrt(jnp.sqrt(jnp.sum(normal * normal)))

        def step(_, value):
            own = halves(value)
            inner = product3(own, own)
            return 1.5 * value - 0.5 * product3(own, halves(inner))

        product = lax.fori_loop(0, POLAR, step, scaled, unroll=4)
    return product


def send(source, target, semaphores, index, device):
    copy = pltpu.make_async_remote_copy(
        src_ref=source,
        dst_ref=target,
        send_sem=semaphores[0].at[index],
        recv_sem=semaphores[1].at[index],
        device_id=device,
        device_id_type=MESH,
    )
    copy.start()
    return copy


def solve_kernel(n, n_pair, final, corner, edge, gram, basis, *refs):
    if final:
        squares_ref, total_ref = refs[:2]
        refs = refs[2:]
    packed, arrived, sums, both, send1, recv1, send2, recv2, send3, recv3 = refs[:10]
    block = corner.shape[0]
    upper = block // 2
    me = lax.axis_index("row")
    core, chip, n_chips = lax.rem(me, 2), me // 2, n // 2
    twin = me + 1 - 2 * core
    chips = [lax.rem(chip + k, n_chips) for k in range(1, n_chips)]
    peers = [2 * other + core for other in chips]
    pair = lax.axis_index("pair")
    slots = [lax.rem(pair + k, n_pair) for k in range(1, n_pair)] if final else []

    barrier = pltpu.get_barrier_semaphore()
    for other in [twin] + peers:
        pl.semaphore_signal(barrier, inc=1, device_id={"row": other}, device_id_type=MESH)
    for slot in slots:
        pl.semaphore_signal(barrier, inc=1, device_id={"pair": slot}, device_id_type=MESH)
    packed[0, :block] = corner[...]
    packed[0, block:] = edge[:upper]
    packed[1, :block] = edge[block:]
    packed[1, block:] = edge[upper:block]
    pl.semaphore_wait(barrier, n_chips + len(slots))

    first = send(packed.at[1 - core], arrived, (send1, recv1), 0, {"row": twin})
    first.wait_recv()
    sums[chip] = packed[core] + arrived[...]
    copies = []
    for k, peer in enumerate(peers):
        copies.append(send(sums.at[chip], sums.at[chip], (send2, recv2), k, {"row": peer}))
    for copy in copies:
        copy.wait_recv()
    total = sums[0]
    for k in range(1, n_chips):
        total = total + sums[k]
    both[core] = total
    last = send(both.at[core], both.at[core], (send3, recv3), 0, {"row": twin})
    last.wait_recv()
    for copy in [first, last] + copies:
        copy.wait_send()
    cross = jnp.concatenate([both[0, block:], both[1, block:]], axis=0)
    gram[:block, :block] = both[0, :block]
    gram[block:, block:] = both[1, :block]
    gram[:block, block:] = cross
    gram[block:, :block] = cross.T
    own = gram[...]
    solved = iterate(own)
    basis[...] = solved
    if not final:
        return
    squares = jnp.sum(solved * product3(halves(own), halves(solved)), axis=0, keepdims=True)
    squares_ref[...] = squares
    sent, landed, send4, recv4 = refs[10:]
    sent[...] = jnp.broadcast_to(jnp.sum(squares), sent.shape)
    traces = []
    for k, slot in enumerate(slots):
        traces.append(send(sent, landed.at[k], (send4, recv4), k, {"pair": slot}))
    value = sent[...]
    for k, copy in enumerate(traces):
        copy.wait_recv()
        value = value + landed[k]
    total_ref[...] = value
    for copy in traces:
        copy.wait_send()


def solve(corner, edge, final):
    n, n_pair = lax.axis_size("row"), lax.axis_size("pair")
    order = edge.shape[0]
    one, many = pltpu.SemaphoreType.DMA((1,)), pltpu.SemaphoreType.DMA((n // 2 - 1,))
    share = (order * 3 // 4, order // 2)
    vmem = pl.BlockSpec(memory_space=pltpu.VMEM)
    shapes = [jax.ShapeDtypeStruct((order, order), jnp.float32)] * 2
    scratch = [
        pltpu.VMEM((2, *share), jnp.float32),
        pltpu.VMEM(share, jnp.float32),
        pltpu.VMEM((n // 2, *share), jnp.float32),
        pltpu.VMEM((2, *share), jnp.float32),
        one,
        one,
        many,
        many,
        one,
        one,
    ]
    if final:
        shapes += [
            jax.ShapeDtypeStruct((1, order), jnp.float32),
            jax.ShapeDtypeStruct((8, 128), jnp.float32),
        ]
        far = pltpu.SemaphoreType.DMA((n_pair - 1,))
        scratch += [
            pltpu.VMEM((8, 128), jnp.float32),
            pltpu.VMEM((n_pair - 1, 8, 128), jnp.float32),
            far,
            far,
        ]
    return pl.pallas_call(
        functools.partial(solve_kernel, n, n_pair, final),
        out_shape=shapes,
        in_specs=[vmem, vmem],
        out_specs=[vmem] * len(shapes),
        scratch_shapes=scratch,
        compiler_params=pltpu.CompilerParams(
            collective_id=int(final), has_side_effects=True, vmem_limit_bytes=16 * 1024 * 1024
        ),
        cost_estimate=pl.CostEstimate(
            flops=35 * 6 * order**3, bytes_accessed=40 * 1024 * 1024, transcendentals=0
        ),
    )(corner, edge)


def on_device(weight, move_flags):
    half_width = weight.shape[1] // 2
    row_count = weight.shape[0] * lax.axis_size("row")
    cell_count = row_count * weight.shape[1] * lax.axis_size("pair")
    head_rows = weight.shape[0] * 10 // 32
    pieces = [weight[:head_rows], weight[head_rows:]]
    part = contract(weight, weight)
    corner, edge = part[:half_width, :half_width], part[:, half_width:]
    for round_index in range(ROUNDS):
        final = round_index + 1 == ROUNDS
        if not final:
            behind = from_behind(pieces[0], "pair", 1)
        gram, basis, *sums = solve(corner, edge, final)
        if final:
            break
        basis, behind = lax.optimization_barrier((basis, behind))
        lead, tail = basis[:, :half_width], basis[:, half_width:]
        lead_moves = move_flags[round_index, 0] == 1
        mover = jnp.where(lead_moves, lead, tail)
        stayer = jnp.where(lead_moves, tail, lead)
        mover_behind = from_behind(mover, "pair", 1)
        coming = from_behind(times(pieces[1], mover), "pair", 1)
        stays = [times(piece, stayer) for piece in pieces]
        corner = contract(stays[0], stays[0]) + contract(stays[1], stays[1])
        head = jnp.concatenate([stays[0], times(behind, mover_behind)], axis=1)
        edge = contract(head, head[:, half_width:])
        rest = jnp.concatenate([stays[1], coming], axis=1)
        edge = edge + contract(rest, coming)
        pieces = [head, rest]
    squares, squares_total = sums[0][0], sums[1][0, 0]
    divisor = jnp.sqrt(squares_total / cell_count)
    current = jnp.concatenate(pieces, axis=0)
    columns = times(current, basis) / divisor
    norm_ratios = jnp.sqrt(squares / row_count) / divisor
    return (columns, norm_ratios)


def solution(mesh):
    return jax.shard_map(
        on_device,
        mesh=mesh,
        in_specs=(P("row", "pair"), P(None, "pair")),
        out_specs=(P("row", "pair"), P("pair")),
        check_vma=False,
    )
```

profile of v0, /device:TPU:0, one launch (start us, length us, event | category | flops | bytes accessed | tf_op | source)
XLA Modules:
  0.0 161.9 jit_solution(12526230836943186812)
XLA Ops:
  0.6 1.3 slice.36
  2.0 3.0 %collective-permute-start = (f32[1120,256]{1,0:T(8,128)S(1)}, f32[1120,256]{1,0:T(8,128)S(1)}, u32[]{:S(2)}, u32[]{:S(2)}) collective-permute-start(f32[1120,256]{1,0:T(8,128)S(1)} %slice.36), channel_id=1, source_target_pairs={{7,0},{0,1},{1,2},{2,3},{3,4},{4,5},{5,6},{6,7},{15,8},{8,9},{9,10... | collective-permute-start | bytes 3440648 | tf_op jit(solution)/shard_map/ppermute | solution.py:21
  5.0 6.2 %fusion.36 = f32[256,256]{1,0:T(8,128)S(1)} fusion(f32[3584,256]{1,0:T(8,128)} %param.2), kind=kOutput, calls=%fused_computation.45 | convolution fusion | flops 1409286144 | bytes 3932160 | tf_op jit(solution)/shard_map/dot_general | solution.py:25
  13.1 19.3 %shard_map.41 = (f32[256,256]{1,0:T(8,128)}, f32[256,256]{1,0:T(8,128)S(1)}) custom-call(f32[128,128]{1,0:T(8,128)S(1)} %slice.44.corner, f32[256,128]{1,0:T(8,128)S(1)} %slice.45.edge), custom_call_target="tpu_custom_call" | custom-call | flops 3523215360 | bytes 41943040 | tf_op jit(solution)/shard_map/pallas_call | solution.py:179
  33.3 1.2 fusion.12
  35.3 1.2 convolution_bitcast_fusion
  37.1 1.6 collective-permute-start.2
  38.7 3.6 %collective-permute-done.1 = f32[256,128]{1,0:T(8,128)S(1)} collective-permute-done((f32[256,128]{1,0:T(8,128)S(1)}, f32[256,128]{1,0:T(8,128)S(1)}, u32[]{:S(2)}, u32[]{:S(2)}) %collective-permute-start.1) | collective-permute-done | bytes 131104 | tf_op jit(solution)/shard_map/ppermute | solution.py:21
  43.2 1.2 fusion.38
  45.1 1.2 fusion.34
  46.3 24.1 %collective-permute-done.2 = f32[2464,128]{1,0:T(8,128)S(1)} collective-permute-done((f32[2464,128]{1,0:T(8,128)S(1)}, f32[2464,128]{1,0:T(8,128)S(1)}, u32[]{:S(2)}, u32[]{:S(2)}) %collective-permute-start.2) | collective-permute-done | bytes 1261600 | tf_op jit(solution)/shard_map/ppermute | solution.py:21
  70.5 2.3 %fusion.21.edge = f32[256,128]{1,0:T(8,128)S(1)} fusion(f32[256,128]{1,0:T(8,128)S(1)} %fusion.34, f32[2464,128]{1,0:T(8,128)S(1)} %collective-permute-done.2, f32[2464,128]{1,0:T(8,128)S(1)} %bitcast.29), kind=kOutput, calls=%fused_computation.25 | convolution fusion | flops 485105664 | bytes 2785280 | tf_op jit(solution)/shard_map/dot_general | solution.py:25
  72.7 18.9 %shard_map.42 = (f32[256,256]{1,0:T(8,128)}, f32[256,256]{1,0:T(8,128)S(1)}) custom-call(f32[128,128]{1,0:T(8,128)S(1)} %convolution_add_fusion.1.corner, f32[256,128]{1,0:T(8,128)S(1)} %fusion.21.edge), custom_call_target="tpu_custom_call" | custom-call | flops 3523215360 | bytes 41943040 | tf_op jit(solution)/shard_map/pallas_call | solution.py:179
  91.6 2.6 %collective-permute-done.3 = f32[1120,256]{1,0:T(8,128)S(1)} collective-permute-done((f32[1120,256]{1,0:T(8,128)S(1)}, f32[1120,256]{1,0:T(8,128)S(1)}, u32[]{:S(2)}, u32[]{:S(2)}) %collective-permute-start.3) | collective-permute-done | bytes 1146912 | tf_op jit(solution)/shard_map/ppermute | solution.py:21
  94.2 1.2 fusion.14
  95.4 1.5 collective-permute-start.5
  96.9 1.2 fusion.15
  98.7 1.2 fusion.40
  100.6 2.7 %collective-permute-done.4 = f32[256,128]{1,0:T(8,128)S(1)} collective-permute-done((f32[256,128]{1,0:T(8,128)S(1)}, f32[256,128]{1,0:T(8,128)S(1)}, u32[]{:S(2)}, u32[]{:S(2)}) %collective-permute-start.4) | collective-permute-done | bytes 131104 | tf_op jit(solution)/shard_map/ppermute | solution.py:21
  103.9 1.2 fusion.17
  105.1 23.5 %collective-permute-done.5 = f32[2464,128]{1,0:T(8,128)S(1)} collective-permute-done((f32[2464,128]{1,0:T(8,128)S(1)}, f32[2464,128]{1,0:T(8,128)S(1)}, u32[]{:S(2)}, u32[]{:S(2)}) %collective-permute-start.5) | collective-permute-done | bytes 1261600 | tf_op jit(solution)/shard_map/ppermute | solution.py:21
  128.6 2.3 %fusion.22.edge = f32[256,128]{1,0:T(8,128)S(1)} fusion(f32[256,128]{1,0:T(8,128)S(1)} %fusion.17, f32[2464,128]{1,0:T(8,128)S(1)} %collective-permute-done.5, f32[2464,128]{1,0:T(8,128)S(1)} %fusion.15), kind=kOutput, calls=%fused_computation.26 | convolution fusion | flops 485105664 | bytes 2785280 | tf_op jit(solution)/shard_map/dot_general | solution.py:25
  130.9 25.7 %shard_map.43 = (f32[256,256]{1,0:T(8,128)}, f32[256,256]{1,0:T(8,128)S(1)}, f32[1,256]{1,0:T(1,128)S(1)}, f32[8,128]{1,0:T(8,128)S(1)}) custom-call(f32[128,128]{1,0:T(8,128)S(1)} %convolution_add_fusion.corner, f32[256,128]{1,0:T(8,128)S(1)} %fusion.22.edge), custom_call_target="tpu_custom_call" | custom-call | flops 3523215360 | bytes 41943040 | tf_op jit(solution)/shard_map/pallas_call | solution.py:179
  158.4 3.4 %convolution_divide_fusion = f32[3584,256]{1,0:T(8,128)} fusion(f32[256,256]{1,0:T(8,128)S(1)} %get-tuple-element.17, f32[2464,128]{1,0:T(8,128)S(1)} %collective-permute-done.5, f32[2464,128]{1,0:T(8,128)S(1)} %fusion.15, f32[1120,128]{1,0:T(8,128)S(1)} %fusion.39, f32[1120,128]{1,0:T(8,128)S(1)} %fusion.26, f32[]{:T(128)} %bitcast.5), kind=kOutput, calls=%fused_computation | convolution fusion | flops 1412956160 | bytes 7602180 | tf_op jit(solution)/shard_map/dot_general | solution.py:31
  (22 shorter events, 7.5 us)
Async XLA Ops:
  2.0 9.2 %copy-start.1 = (s32[2,1]{0,1:T(1,128)S(1)}, s32[2,1]{0,1:T(1,128)}, u32[]{:S(2)}) copy-start(s32[2,1]{0,1:T(1,128)} %param.3) | copy-start | bytes 28
  2.0 31.3 %collective-permute-start = (f32[1120,256]{1,0:T(8,128)S(1)}, f32[1120,256]{1,0:T(8,128)S(1)}, u32[]{:S(2)}, u32[]{:S(2)}) collective-permute-start(f32[1120,256]{1,0:T(8,128)S(1)} %slice.36), channel_id=1, source_target_pairs={{7,0},{0,1},{1,2},{2,3},{3,4},{4,5},{5,6},{6,7},{15,8},{8,9},{9,10... | collective-permute-start | bytes 3440648 | tf_op jit(solution)/shard_map/ppermute | solution.py:21
  13.1 20.2 %copy-start = (f32[3584,256]{1,0:T(8,128)S(1)}, f32[3584,256]{1,0:T(8,128)}, u32[]{:S(2)}) copy-start(f32[3584,256]{1,0:T(8,128)} %param.2) | copy-start | bytes 11010052
  34.5 7.7 %collective-permute-start.1 = (f32[256,128]{1,0:T(8,128)S(1)}, f32[256,128]{1,0:T(8,128)S(1)}, u32[]{:S(2)}, u32[]{:S(2)}) collective-permute-start(f32[256,128]{1,0:T(8,128)S(1)} %slice_select_fusion.2), channel_id=1, source_target_pairs={{7,0},{0,1},{1,2},{2,3},{3,4},{4,5},{5,6},{6,7},{15,8},{8,9},{9,10... | collective-permute-start | bytes 393224 | tf_op jit(solution)/shard_map/ppermute | solution.py:21
  37.1 33.3 %collective-permute-start.2 = (f32[2464,128]{1,0:T(8,128)S(1)}, f32[2464,128]{1,0:T(8,128)S(1)}, u32[]{:S(2)}, u32[]{:S(2)}) collective-permute-start(f32[2464,128]{1,0:T(8,128)S(1)} %convolution_bitcast_fusion), channel_id=1, source_target_pairs={{7,0},{0,1},{1,2},{2,3},{3,4},{4,5},{5,6},{6,7},{15,8},{8,9},{9,10... | collective-permute-start | bytes 3784712 | tf_op jit(solution)/shard_map/ppermute | solution.py:21
  43.0 51.2 %collective-permute-start.3 = (f32[1120,256]{1,0:T(8,128)S(1)}, f32[1120,256]{1,0:T(8,128)S(1)}, u32[]{:S(2)}, u32[]{:S(2)}) collective-permute-start(f32[1120,256]{1,0:T(8,128)S(1)} %pad_maximum_fusion.4), channel_id=1, source_target_pairs={{7,0},{0,1},{1,2},{2,3},{3,4},{4,5},{5,6},{6,7},{15,8},{8,9},{9,10... | collective-permute-start | bytes 3440648 | tf_op jit(solution)/shard_map/ppermute | solution.py:21
  94.2 9.1 %collective-permute-start.4 = (f32[256,128]{1,0:T(8,128)S(1)}, f32[256,128]{1,0:T(8,128)S(1)}, u32[]{:S(2)}, u32[]{:S(2)}) collective-permute-start(f32[256,128]{1,0:T(8,128)S(1)} %slice_select_fusion), channel_id=1, source_target_pairs={{7,0},{0,1},{1,2},{2,3},{3,4},{4,5},{5,6},{6,7},{15,8},{8,9},{9,10... | collective-permute-start | bytes 393224 | tf_op jit(solution)/shard_map/ppermute | solution.py:21
  95.4 33.2 %collective-permute-start.5 = (f32[2464,128]{1,0:T(8,128)S(1)}, f32[2464,128]{1,0:T(8,128)S(1)}, u32[]{:S(2)}, u32[]{:S(2)}) collective-permute-start(f32[2464,128]{1,0:T(8,128)S(1)} %fusion.14), channel_id=1, source_target_pairs={{7,0},{0,1},{1,2},{2,3},{3,4},{4,5},{5,6},{6,7},{15,8},{8,9},{9,10... | collective-permute-start | bytes 3784712 | tf_op jit(solution)/shard_map/ppermute | solution.py:21
where the time goes:
time: 162 us
  Pallas kernels  63.9 us (39%)
  waiting for transfers between devices  57.3 us (35%)
  matrix products  27.5 us (17%)
  starting transfers between devices  7.12 us (4%)
  between operations  2.84 us (2%)
  local copies, waits for them, and re-layouts  2.46 us (2%)
    pallas_call x3, Pallas kernels, solve(): pl.pallas_call(functools.partial(solve_kernel, n, n_pair, final), out_sha...  63.9 us
    ppermute x6, waiting for transfers between devices, from_behind(): return lax.ppermute(block, axis, route)  57.3 us
    dot_general x9, matrix products, contract(): lax.dot_general(left, right, (((0,), (0,)), ((), ())), precision=precise,...  16.9 us
    dot_general x9, matrix products, times(): jnp.dot(left, right, precision=precise, preferred_element_type=jnp.float32)  10.7 us
    ppermute x6, starting transfers between devices, from_behind(): return lax.ppermute(block, axis, route)  7.12 us
  transfers between devices with their start and end apart: 6, of which 6 were waited for; matrix products, arithmetic and copies ran while one was open for 13% of the time, Pallas kernels for 24%

commit v1 on v0

--- a/solution.py
+++ b/solution.py
@@ -77,10 +77,10 @@
     return copy
 
 
-def solve_kernel(n, n_pair, final, corner, edge, gram, basis, *refs):
+def solve_kernel(n, n_pair, final, counts, corner, edge, gram, basis, *refs):
     if final:
-        squares_ref, total_ref = refs[:2]
-        refs = refs[2:]
+        norms_ref = refs[0]
+        refs = refs[1:]
     packed, arrived, sums, both, send1, recv1, send2, recv2, send3, recv3 = refs[:10]
     block = corner.shape[0]
     upper = block // 2
@@ -126,11 +126,10 @@
     gram[block:, :block] = cross.T
     own = gram[...]
     solved = iterate(own)
-    basis[...] = solved
     if not final:
+        basis[...] = solved
         return
     squares = jnp.sum(solved * product3(halves(own), halves(solved)), axis=0, keepdims=True)
-    squares_ref[...] = squares
     sent, landed, send4, recv4 = refs[10:]
     sent[...] = jnp.broadcast_to(jnp.sum(squares), sent.shape)
     traces = []
@@ -140,12 +139,15 @@
     for k, copy in enumerate(traces):
         copy.wait_recv()
         value = value + landed[k]
-    total_ref[...] = value
+    row_count, cell_count = counts
+    divisor = jnp.sqrt(value[:1, :1] / cell_count)
+    basis[...] = solved / divisor
+    norms_ref[...] = jnp.sqrt(squares / row_count) / divisor
     for copy in traces:
         copy.wait_send()
 
 
-def solve(corner, edge, final):
+def solve(corner, edge, final, counts):
     n, n_pair = lax.axis_size("row"), lax.axis_size("pair")
     order = edge.shape[0]
     one, many = pltpu.SemaphoreType.DMA((1,)), pltpu.SemaphoreType.DMA((n // 2 - 1,))
@@ -165,10 +167,7 @@
         one,
     ]
     if final:
-        shapes += [
-            jax.ShapeDtypeStruct((1, order), jnp.float32),
-            jax.ShapeDtypeStruct((8, 128), jnp.float32),
-        ]
+        shapes += [jax.ShapeDtypeStruct((1, order), jnp.float32)]
         far = pltpu.SemaphoreType.DMA((n_pair - 1,))
         scratch += [
             pltpu.VMEM((8, 128), jnp.float32),
@@ -177,7 +176,7 @@
             far,
         ]
     return pl.pallas_call(
-        functools.partial(solve_kernel, n, n_pair, final),
+        functools.partial(solve_kernel, n, n_pair, final, counts),
         out_shape=shapes,
         in_specs=[vmem, vmem],
         out_specs=[vmem] * len(shapes),
@@ -194,8 +193,8 @@
 def on_device(weight, move_flags):
     half_width = weight.shape[1] // 2
     row_count = weight.shape[0] * lax.axis_size("row")
-    cell_count = row_count * weight.shape[1] * lax.axis_size("pair")
-    head_rows = weight.shape[0] * 10 // 32
+    counts = (row_count, row_count * weight.shape[1] * lax.axis_size("pair"))
+    head_rows = weight.shape[0] * 11 // 32
     pieces = [weight[:head_rows], weight[head_rows:]]
     part = contract(weight, weight)
     corner, edge = part[:half_width, :half_width], part[:, half_width:]
@@ -203,16 +202,16 @@
         final = round_index + 1 == ROUNDS
         if not final:
             behind = from_behind(pieces[0], "pair", 1)
-        gram, basis, *sums = solve(corner, edge, final)
+        gram, basis, *sums = solve(corner, edge, final, counts)
         if final:
             break
-        basis, behind = lax.optimization_barrier((basis, behind))
         lead, tail = basis[:, :half_width], basis[:, half_width:]
         lead_moves = move_flags[round_index, 0] == 1
         mover = jnp.where(lead_moves, lead, tail)
         stayer = jnp.where(lead_moves, tail, lead)
         mover_behind = from_behind(mover, "pair", 1)
-        coming = from_behind(times(pieces[1], mover), "pair", 1)
+        moving, behind = lax.optimization_barrier((times(pieces[1], mover), behind))
+        coming = from_behind(moving, "pair", 1)
         stays = [times(piece, stayer) for piece in pieces]
         corner = contract(stays[0], stays[0]) + contract(stays[1], stays[1])
         head = jnp.concatenate([stays[0], times(behind, mover_behind)], axis=1)
@@ -220,11 +219,8 @@
         rest = jnp.concatenate([stays[1], coming], axis=1)
         edge = edge + contract(rest, coming)
         pieces = [head, rest]
-    squares, squares_total = sums[0][0], sums[1][0, 0]
-    divisor = jnp.sqrt(squares_total / cell_count)
-    current = jnp.concatenate(pieces, axis=0)
-    columns = times(current, basis) / divisor
-    norm_ratios = jnp.sqrt(squares / row_count) / divisor
+    columns = times(jnp.concatenate(pieces, axis=0), basis)
+    norm_ratios = sums[0][0]
     return (columns, norm_ratios)
 
 

time: 162 us -> 157 us (0.969)
  waiting for transfers between devices: 57.3 us -> 54.1 us
    ppermute x6, waiting for transfers between devices: 57.3 us -> 54.1 us  [from_behind(): return lax.ppermute(block, axis, route)]
  transfers between devices with their start and end apart: 6 -> 6, of which waited for: 6 -> 4; matrix products, arithmetic and copies ran while one was open for 13% -> 14% of each run, Pallas kernels for 24% -> 24%
where the time goes in v1:
time: 157 us
  Pallas kernels  62.7 us (40%)
  waiting for transfers between devices  54.1 us (34%)
  matrix products  27.5 us (18%)
  starting transfers between devices  7.99 us (5%)
  local copies, waits for them, and re-layouts  2.56 us (2%)
  between operations  2.16 us (1%)
    pallas_call x3, Pallas kernels, solve(): pl.pallas_call(functools.partial(solve_kernel, n, n_pair, final, counts),...  62.7 us
    ppermute x6, waiting for transfers between devices, from_behind(): return lax.ppermute(block, axis, route)  54.1 us
    dot_general x9, matrix products, contract(): lax.dot_general(left, right, (((0,), (0,)), ((), ())), precision=precise,...  16.8 us
    dot_general x9, matrix products, times(): jnp.dot(left, right, precision=precise, preferred_element_type=jnp.float32)  10.7 us
    ppermute x6, starting transfers between devices, from_behind(): return lax.ppermute(block, axis, route)  7.99 us
  transfers between devices with their start and end apart: 6, of which 4 were waited for; matrix products, arithmetic and copies ran while one was open for 14% of the time, Pallas kernels for 24%

profile of v1, /device:TPU:0, one launch (start us, length us, event | category | flops | bytes accessed | tf_op | source)
XLA Modules:
  0.0 157.1 jit_solution(6504611356083000631)
XLA Ops:
  0.6 1.4 slice.35
  2.0 3.0 %collective-permute-start = (f32[1232,256]{1,0:T(8,128)S(1)}, f32[1232,256]{1,0:T(8,128)S(1)}, u32[]{:S(2)}, u32[]{:S(2)}) collective-permute-start(f32[1232,256]{1,0:T(8,128)S(1)} %slice.35), channel_id=1, source_target_pairs={{7,0},{0,1},{1,2},{2,3},{3,4},{4,5},{5,6},{6,7},{15,8},{8,9},{9,10... | collective-permute-start | bytes 3784712 | tf_op jit(solution)/shard_map/ppermute | solution.py:21
  5.0 6.2 %fusion.37 = f32[256,256]{1,0:T(8,128)S(1)} fusion(f32[3584,256]{1,0:T(8,128)} %param.2), kind=kOutput, calls=%fused_computation.44 | convolution fusion | flops 1409286144 | bytes 3932160 | tf_op jit(solution)/shard_map/dot_general | solution.py:25
  11.3 19.3 %shard_map.41 = (f32[256,256]{1,0:T(8,128)}, f32[256,256]{1,0:T(8,128)S(1)}) custom-call(f32[128,128]{1,0:T(8,128)S(1)} %slice.40.corner, f32[256,128]{1,0:T(8,128)S(1)} %slice.41.edge), custom_call_target="tpu_custom_call" | custom-call | flops 3523215360 | bytes 41943040 | tf_op jit(solution)/shard_map/pallas_call | solution.py:178
  31.9 1.6 %collective-permute-start.1 = (f32[256,128]{1,0:T(8,128)S(1)}, f32[256,128]{1,0:T(8,128)S(1)}, u32[]{:S(2)}, u32[]{:S(2)}) collective-permute-start(f32[256,128]{1,0:T(8,128)S(1)} %slice_select_fusion.2), channel_id=1, source_target_pairs={{7,0},{0,1},{1,2},{2,3},{3,4},{4,5},{5,6},{6,7},{15,8},{8,9},{9,10... | collective-permute-start | bytes 393224 | tf_op jit(solution)/shard_map/ppermute | solution.py:21
  34.1 1.2 fusion.12
  35.3 1.2 fusion.39
  36.5 1.2 convolution_bitcast_fusion
  37.6 1.8 %collective-permute-start.2 = (f32[2352,128]{1,0:T(8,128)S(1)}, f32[2352,128]{1,0:T(8,128)S(1)}, u32[]{:S(2)}, u32[]{:S(2)}) collective-permute-start(f32[2352,128]{1,0:T(8,128)S(1)} %convolution_bitcast_fusion), channel_id=1, source_target_pairs={{7,0},{0,1},{1,2},{2,3},{3,4},{4,5},{5,6},{6,7},{15,8},{8,9},{9,10... | collective-permute-start | bytes 3612680 | tf_op jit(solution)/shard_map/ppermute | solution.py:21
  40.1 0.7 convolution_add_fusion.1.corner
  41.6 1.6 %collective-permute-start.3 = (f32[1232,256]{1,0:T(8,128)S(1)}, f32[1232,256]{1,0:T(8,128)S(1)}, u32[]{:S(2)}, u32[]{:S(2)}) collective-permute-start(f32[1232,256]{1,0:T(8,128)S(1)} %pad_maximum_fusion.4), channel_id=1, source_target_pairs={{7,0},{0,1},{1,2},{2,3},{3,4},{4,5},{5,6},{6,7},{15,8},{8,9},{9,10... | collective-permute-start | bytes 3784712 | tf_op jit(solution)/shard_map/ppermute | solution.py:21
  43.2 1.2 fusion.35
  44.4 25.5 %collective-permute-done.2 = f32[2352,128]{1,0:T(8,128)S(1)} collective-permute-done((f32[2352,128]{1,0:T(8,128)S(1)}, f32[2352,128]{1,0:T(8,128)S(1)}, u32[]{:S(2)}, u32[]{:S(2)}) %collective-permute-start.2) | collective-permute-done | bytes 1204256 | tf_op jit(solution)/shard_map/ppermute | solution.py:21
  69.9 2.2 %fusion.22.edge = f32[256,128]{1,0:T(8,128)S(1)} fusion(f32[256,128]{1,0:T(8,128)S(1)} %fusion.35, f32[2352,128]{1,0:T(8,128)S(1)} %collective-permute-done.2, f32[2352,128]{1,0:T(8,128)S(1)} %bitcast.29), kind=kOutput, calls=%fused_computation.25 | convolution fusion | flops 463056896 | bytes 2670592 | tf_op jit(solution)/shard_map/dot_general | solution.py:25
  72.1 18.8 %shard_map.42 = (f32[256,256]{1,0:T(8,128)}, f32[256,256]{1,0:T(8,128)S(1)}) custom-call(f32[128,128]{1,0:T(8,128)S(1)} %convolution_add_fusion.1.corner, f32[256,128]{1,0:T(8,128)S(1)} %fusion.22.edge), custom_call_target="tpu_custom_call" | custom-call | flops 3523215360 | bytes 41943040 | tf_op jit(solution)/shard_map/pallas_call | solution.py:178
  91.1 1.1 fusion.15
  92.2 1.1 fusion.16
  93.3 2.8 %collective-permute-done.3 = f32[1232,256]{1,0:T(8,128)S(1)} collective-permute-done((f32[1232,256]{1,0:T(8,128)S(1)}, f32[1232,256]{1,0:T(8,128)S(1)}, u32[]{:S(2)}, u32[]{:S(2)}) %collective-permute-start.3) | collective-permute-done | bytes 1261600 | tf_op jit(solution)/shard_map/ppermute | solution.py:21
  96.8 1.2 fusion.41
  100.0 1.2 fusion.18
  101.2 25.2 %collective-permute-done.5 = f32[2352,128]{1,0:T(8,128)S(1)} collective-permute-done((f32[2352,128]{1,0:T(8,128)S(1)}, f32[2352,128]{1,0:T(8,128)S(1)}, u32[]{:S(2)}, u32[]{:S(2)}) %collective-permute-start.5) | collective-permute-done | bytes 1204256 | tf_op jit(solution)/shard_map/ppermute | solution.py:21
  126.4 2.2 %fusion.23.edge = f32[256,128]{1,0:T(8,128)S(1)} fusion(f32[256,128]{1,0:T(8,128)S(1)} %fusion.18, f32[2352,128]{1,0:T(8,128)S(1)} %collective-permute-done.5, f32[2352,128]{1,0:T(8,128)S(1)} %fusion.15), kind=kOutput, calls=%fused_computation.26 | convolution fusion | flops 463056896 | bytes 2670592 | tf_op jit(solution)/shard_map/dot_general | solution.py:25
  128.6 24.5 %shard_map.43 = (f32[256,256]{1,0:T(8,128)}, f32[256,256]{1,0:T(8,128)S(1)}, f32[1,256]{1,0:T(1,128)S(1)}) custom-call(f32[128,128]{1,0:T(8,128)S(1)} %convolution_add_fusion.corner, f32[256,128]{1,0:T(8,128)S(1)} %fusion.23.edge), custom_call_target="tpu_custom_call" | custom-call | flops 3523215360 | bytes 41943040 | tf_op jit(solution)/shard_map/pallas_call | solution.py:178
  153.1 3.4 %fusion = f32[3584,256]{1,0:T(8,128)} fusion(f32[256,256]{1,0:T(8,128)S(1)} %get-tuple-element.16, f32[2352,128]{1,0:T(8,128)S(1)} %collective-permute-done.5, f32[2352,128]{1,0:T(8,128)S(1)} %fusion.15, f32[1232,128]{1,0:T(8,128)S(1)} %fusion.40, f32[1232,128]{1,0:T(8,128)S(1)} %fusion.27), kind=kOutput, calls=%fused_computation.1 | convolution fusion | flops 1412038656 | bytes 7602176 | tf_op jit(solution)/shard_map/dot_general | solution.py:31
  (21 shorter events, 5.4 us)
Async XLA Ops:
  2.0 35.6 %collective-permute-start = (f32[1232,256]{1,0:T(8,128)S(1)}, f32[1232,256]{1,0:T(8,128)S(1)}, u32[]{:S(2)}, u32[]{:S(2)}) collective-permute-start(f32[1232,256]{1,0:T(8,128)S(1)} %slice.35), channel_id=1, source_target_pairs={{7,0},{0,1},{1,2},{2,3},{3,4},{4,5},{5,6},{6,7},{15,8},{8,9},{9,10... | collective-permute-start | bytes 3784712 | tf_op jit(solution)/shard_map/ppermute | solution.py:21
  11.2 19.3 %copy-start.1 = (s32[2,1]{0,1:T(1,128)S(1)}, s32[2,1]{0,1:T(1,128)}, u32[]{:S(2)}) copy-start(s32[2,1]{0,1:T(1,128)} %param.3) | copy-start | bytes 28
  11.3 22.8 %copy-start = (f32[3584,256]{1,0:T(8,128)S(1)}, f32[3584,256]{1,0:T(8,128)}, u32[]{:S(2)}) copy-start(f32[3584,256]{1,0:T(8,128)} %param.2) | copy-start | bytes 11010052
  31.9 9.0 %collective-permute-start.1 = (f32[256,128]{1,0:T(8,128)S(1)}, f32[256,128]{1,0:T(8,128)S(1)}, u32[]{:S(2)}, u32[]{:S(2)}) collective-permute-start(f32[256,128]{1,0:T(8,128)S(1)} %slice_select_fusion.2), channel_id=1, source_target_pairs={{7,0},{0,1},{1,2},{2,3},{3,4},{4,5},{5,6},{6,7},{15,8},{8,9},{9,10... | collective-permute-start | bytes 393224 | tf_op jit(solution)/shard_map/ppermute | solution.py:21
  37.6 32.3 %collective-permute-start.2 = (f32[2352,128]{1,0:T(8,128)S(1)}, f32[2352,128]{1,0:T(8,128)S(1)}, u32[]{:S(2)}, u32[]{:S(2)}) collective-permute-start(f32[2352,128]{1,0:T(8,128)S(1)} %convolution_bitcast_fusion), channel_id=1, source_target_pairs={{7,0},{0,1},{1,2},{2,3},{3,4},{4,5},{5,6},{6,7},{15,8},{8,9},{9,10... | collective-permute-start | bytes 3612680 | tf_op jit(solution)/shard_map/ppermute | solution.py:21
  41.6 54.5 %collective-permute-start.3 = (f32[1232,256]{1,0:T(8,128)S(1)}, f32[1232,256]{1,0:T(8,128)S(1)}, u32[]{:S(2)}, u32[]{:S(2)}) collective-permute-start(f32[1232,256]{1,0:T(8,128)S(1)} %pad_maximum_fusion.4), channel_id=1, source_target_pairs={{7,0},{0,1},{1,2},{2,3},{3,4},{4,5},{5,6},{6,7},{15,8},{8,9},{9,10... | collective-permute-start | bytes 3784712 | tf_op jit(solution)/shard_map/ppermute | solution.py:21
  91.0 8.3 %collective-permute-start.4 = (f32[256,128]{1,0:T(8,128)S(1)}, f32[256,128]{1,0:T(8,128)S(1)}, u32[]{:S(2)}, u32[]{:S(2)}) collective-permute-start(f32[256,128]{1,0:T(8,128)S(1)} %slice_select_fusion), channel_id=1, source_target_pairs={{7,0},{0,1},{1,2},{2,3},{3,4},{4,5},{5,6},{6,7},{15,8},{8,9},{9,10... | collective-permute-start | bytes 393224 | tf_op jit(solution)/shard_map/ppermute | solution.py:21
  96.1 30.3 %collective-permute-start.5 = (f32[2352,128]{1,0:T(8,128)S(1)}, f32[2352,128]{1,0:T(8,128)S(1)}, u32[]{:S(2)}, u32[]{:S(2)}) collective-permute-start(f32[2352,128]{1,0:T(8,128)S(1)} %fusion.16), channel_id=1, source_target_pairs={{7,0},{0,1},{1,2},{2,3},{3,4},{4,5},{5,6},{6,7},{15,8},{8,9},{9,10... | collective-permute-start | bytes 3612680 | tf_op jit(solution)/shard_map/ppermute | solution.py:21

commit v2 on v1

--- a/solution.py
+++ b/solution.py
@@ -196,8 +196,8 @@
     counts = (row_count, row_count * weight.shape[1] * lax.axis_size("pair"))
     head_rows = weight.shape[0] * 11 // 32
     pieces = [weight[:head_rows], weight[head_rows:]]
-    part = contract(weight, weight)
-    corner, edge = part[:half_width, :half_width], part[:, half_width:]
+    first, second = weight[:, :half_width], weight[:, half_width:]
+    corner, edge = contract(first, first), contract(weight, second)
     for round_index in range(ROUNDS):
         final = round_index + 1 == ROUNDS
         if not final:

time: 157 us -> 158 us (level)
    dot_general x9 -> x10, matrix products: 16.8 us -> 17.3 us  [contract(): lax.dot_general(left, right, (((0,), (0,)), ((), ())), precision=precise,...]
  transfers between devices with their start and end apart: 6 -> 6, of which waited for: 4 -> 4; matrix products, arithmetic and copies ran while one was open for 14% -> 15% of each run, Pallas kernels for 24% -> 24%
where the time goes in v2:
time: 158 us
  Pallas kernels  62.7 us (40%)
  waiting for transfers between devices  54.1 us (34%)
  matrix products  28 us (18%)
  starting transfers between devices  7.99 us (5%)
  local copies, waits for them, and re-layouts  2.69 us (2%)
  between operations  2.14 us (1%)
    pallas_call x3, Pallas kernels, solve(): pl.pallas_call(functools.partial(solve_kernel, n, n_pair, final, counts),...  62.7 us
    ppermute x6, waiting for transfers between devices, from_behind(): return lax.ppermute(block, axis, route)  54.1 us
    dot_general x10, matrix products, contract(): lax.dot_general(left, right, (((0,), (0,)), ((), ())), precision=precise,...  17.3 us
    dot_general x9, matrix products, times(): jnp.dot(left, right, precision=precise, preferred_element_type=jnp.float32)  10.7 us
    ppermute x6, starting transfers between devices, from_behind(): return lax.ppermute(block, axis, route)  7.99 us
  transfers between devices with their start and end apart: 6, of which 4 were waited for; matrix products, arithmetic and copies ran while one was open for 15% of the time, Pallas kernels for 24%

profile of v2, /device:TPU:0, one launch (start us, length us, event | category | flops | bytes accessed | tf_op | source)
XLA Modules:
  0.0 157.8 jit_solution(3169533076829606695)
XLA Ops:
  0.6 1.5 slice.35
  2.2 3.0 %collective-permute-start = (f32[1232,256]{1,0:T(8,128)S(1)}, f32[1232,256]{1,0:T(8,128)S(1)}, u32[]{:S(2)}, u32[]{:S(2)}) collective-permute-start(f32[1232,256]{1,0:T(8,128)S(1)} %slice.35), channel_id=1, source_target_pairs={{7,0},{0,1},{1,2},{2,3},{3,4},{4,5},{5,6},{6,7},{15,8},{8,9},{9,10... | collective-permute-start | bytes 3784712 | tf_op jit(solution)/shard_map/ppermute | solution.py:21
  5.2 3.7 %fusion.20.corner = f32[128,128]{1,0:T(8,128)S(1)} fusion(f32[3584,256]{1,0:T(8,128)} %param.2), kind=kOutput, calls=%fused_computation.22 | convolution fusion | flops 352321536 | bytes 1900544 | tf_op jit(solution)/shard_map/dot_general | solution.py:25
  8.9 3.1 %fusion.18.edge = f32[256,128]{1,0:T(8,128)S(1)} fusion(f32[3584,256]{1,0:T(8,128)S(1)} %copy-done), kind=kOutput, calls=%fused_computation.20 | convolution fusion | flops 704643072 | bytes 5636096 | tf_op jit(solution)/shard_map/dot_general | solution.py:25
  11.9 19.3 %shard_map.41 = (f32[256,256]{1,0:T(8,128)}, f32[256,256]{1,0:T(8,128)S(1)}) custom-call(f32[128,128]{1,0:T(8,128)S(1)} %fusion.20.corner, f32[256,128]{1,0:T(8,128)S(1)} %fusion.18.edge), custom_call_target="tpu_custom_call" | custom-call | flops 3523215360 | bytes 41943040 | tf_op jit(solution)/shard_map/pallas_call | solution.py:178
  32.5 1.6 %collective-permute-start.1 = (f32[256,128]{1,0:T(8,128)S(1)}, f32[256,128]{1,0:T(8,128)S(1)}, u32[]{:S(2)}, u32[]{:S(2)}) collective-permute-start(f32[256,128]{1,0:T(8,128)S(1)} %slice_select_fusion.2), channel_id=1, source_target_pairs={{7,0},{0,1},{1,2},{2,3},{3,4},{4,5},{5,6},{6,7},{15,8},{8,9},{9,10... | collective-permute-start | bytes 393224 | tf_op jit(solution)/shard_map/ppermute | solution.py:21
  34.8 1.2 fusion.12
  35.9 1.2 fusion.42
  37.2 1.2 convolution_bitcast_fusion
  38.3 1.8 %collective-permute-start.2 = (f32[2352,128]{1,0:T(8,128)S(1)}, f32[2352,128]{1,0:T(8,128)S(1)}, u32[]{:S(2)}, u32[]{:S(2)}) collective-permute-start(f32[2352,128]{1,0:T(8,128)S(1)} %convolution_bitcast_fusion), channel_id=1, source_target_pairs={{7,0},{0,1},{1,2},{2,3},{3,4},{4,5},{5,6},{6,7},{15,8},{8,9},{9,10... | collective-permute-start | bytes 3612680 | tf_op jit(solution)/shard_map/ppermute | solution.py:21
  42.3 1.6 collective-permute-start.3
  43.9 1.2 fusion.39
  45.1 25.5 %collective-permute-done.2 = f32[2352,128]{1,0:T(8,128)S(1)} collective-permute-done((f32[2352,128]{1,0:T(8,128)S(1)}, f32[2352,128]{1,0:T(8,128)S(1)}, u32[]{:S(2)}, u32[]{:S(2)}) %collective-permute-start.2) | collective-permute-done | bytes 1204256 | tf_op jit(solution)/shard_map/ppermute | solution.py:21
  70.6 2.2 %fusion.26.edge = f32[256,128]{1,0:T(8,128)S(1)} fusion(f32[256,128]{1,0:T(8,128)S(1)} %fusion.39, f32[2352,128]{1,0:T(8,128)S(1)} %collective-permute-done.2, f32[2352,128]{1,0:T(8,128)S(1)} %bitcast.28), kind=kOutput, calls=%fused_computation.29 | convolution fusion | flops 463056896 | bytes 2670592 | tf_op jit(solution)/shard_map/dot_general | solution.py:25
  72.8 18.8 %shard_map.42 = (f32[256,256]{1,0:T(8,128)}, f32[256,256]{1,0:T(8,128)S(1)}) custom-call(f32[128,128]{1,0:T(8,128)S(1)} %convolution_add_fusion.1.corner, f32[256,128]{1,0:T(8,128)S(1)} %fusion.26.edge), custom_call_target="tpu_custom_call" | custom-call | flops 3523215360 | bytes 41943040 | tf_op jit(solution)/shard_map/pallas_call | solution.py:178
  91.7 1.1 fusion.15
  92.9 1.1 fusion.16
  94.0 2.8 %collective-permute-done.3 = f32[1232,256]{1,0:T(8,128)S(1)} collective-permute-done((f32[1232,256]{1,0:T(8,128)S(1)}, f32[1232,256]{1,0:T(8,128)S(1)}, u32[]{:S(2)}, u32[]{:S(2)}) %collective-permute-start.3) | collective-permute-done | bytes 1261600 | tf_op jit(solution)/shard_map/ppermute | solution.py:21
  97.4 1.2 fusion.44
  100.6 1.2 fusion.22
  101.9 25.2 %collective-permute-done.5 = f32[2352,128]{1,0:T(8,128)S(1)} collective-permute-done((f32[2352,128]{1,0:T(8,128)S(1)}, f32[2352,128]{1,0:T(8,128)S(1)}, u32[]{:S(2)}, u32[]{:S(2)}) %collective-permute-start.5) | collective-permute-done | bytes 1204256 | tf_op jit(solution)/shard_map/ppermute | solution.py:21
  127.1 2.2 %fusion.27.edge = f32[256,128]{1,0:T(8,128)S(1)} fusion(f32[256,128]{1,0:T(8,128)S(1)} %fusion.22, f32[2352,128]{1,0:T(8,128)S(1)} %collective-permute-done.5, f32[2352,128]{1,0:T(8,128)S(1)} %fusion.15), kind=kOutput, calls=%fused_computation.30 | convolution fusion | flops 463056896 | bytes 2670592 | tf_op jit(solution)/shard_map/dot_general | solution.py:25
  129.3 24.5 %shard_map.43 = (f32[256,256]{1,0:T(8,128)}, f32[256,256]{1,0:T(8,128)S(1)}, f32[1,256]{1,0:T(1,128)S(1)}) custom-call(f32[128,128]{1,0:T(8,128)S(1)} %convolution_add_fusion.corner, f32[256,128]{1,0:T(8,128)S(1)} %fusion.27.edge), custom_call_target="tpu_custom_call" | custom-call | flops 3523215360 | bytes 41943040 | tf_op jit(solution)/shard_map/pallas_call | solution.py:178
  153.8 3.4 %fusion = f32[3584,256]{1,0:T(8,128)} fusion(f32[256,256]{1,0:T(8,128)S(1)} %get-tuple-element.16, f32[2352,128]{1,0:T(8,128)S(1)} %collective-permute-done.5, f32[2352,128]{1,0:T(8,128)S(1)} %fusion.15, f32[1232,128]{1,0:T(8,128)S(1)} %fusion.43, f32[1232,128]{1,0:T(8,128)S(1)} %fusion.31), kind=kOutput, calls=%fused_computation.1 | convolution fusion | flops 1412038656 | bytes 7602176 | tf_op jit(solution)/shard_map/dot_general | solution.py:31
  (20 shorter events, 6.1 us)
Async XLA Ops:
  0.6 8.2 %copy-start = (f32[3584,256]{1,0:T(8,128)S(1)}, f32[3584,256]{1,0:T(8,128)}, u32[]{:S(2)}) copy-start(f32[3584,256]{1,0:T(8,128)} %param.2) | copy-start | bytes 11010052
  2.2 36.2 %collective-permute-start = (f32[1232,256]{1,0:T(8,128)S(1)}, f32[1232,256]{1,0:T(8,128)S(1)}, u32[]{:S(2)}, u32[]{:S(2)}) collective-permute-start(f32[1232,256]{1,0:T(8,128)S(1)} %slice.35), channel_id=1, source_target_pairs={{7,0},{0,1},{1,2},{2,3},{3,4},{4,5},{5,6},{6,7},{15,8},{8,9},{9,10... | collective-permute-start | bytes 3784712 | tf_op jit(solution)/shard_map/ppermute | solution.py:21
  11.9 19.3 %copy-start.1 = (s32[2,1]{0,1:T(1,128)S(1)}, s32[2,1]{0,1:T(1,128)}, u32[]{:S(2)}) copy-start(s32[2,1]{0,1:T(1,128)} %param.3) | copy-start | bytes 28
  32.5 9.0 %collective-permute-start.1 = (f32[256,128]{1,0:T(8,128)S(1)}, f32[256,128]{1,0:T(8,128)S(1)}, u32[]{:S(2)}, u32[]{:S(2)}) collective-permute-start(f32[256,128]{1,0:T(8,128)S(1)} %slice_select_fusion.2), channel_id=1, source_target_pairs={{7,0},{0,1},{1,2},{2,3},{3,4},{4,5},{5,6},{6,7},{15,8},{8,9},{9,10... | collective-permute-start | bytes 393224 | tf_op jit(solution)/shard_map/ppermute | solution.py:21
  38.3 32.3 %collective-permute-start.2 = (f32[2352,128]{1,0:T(8,128)S(1)}, f32[2352,128]{1,0:T(8,128)S(1)}, u32[]{:S(2)}, u32[]{:S(2)}) collective-permute-start(f32[2352,128]{1,0:T(8,128)S(1)} %convolution_bitcast_fusion), channel_id=1, source_target_pairs={{7,0},{0,1},{1,2},{2,3},{3,4},{4,5},{5,6},{6,7},{15,8},{8,9},{9,10... | collective-permute-start | bytes 3612680 | tf_op jit(solution)/shard_map/ppermute | solution.py:21
  42.3 54.5 %collective-permute-start.3 = (f32[1232,256]{1,0:T(8,128)S(1)}, f32[1232,256]{1,0:T(8,128)S(1)}, u32[]{:S(2)}, u32[]{:S(2)}) collective-permute-start(f32[1232,256]{1,0:T(8,128)S(1)} %pad_maximum_fusion.4), channel_id=1, source_target_pairs={{7,0},{0,1},{1,2},{2,3},{3,4},{4,5},{5,6},{6,7},{15,8},{8,9},{9,10... | collective-permute-start | bytes 3784712 | tf_op jit(solution)/shard_map/ppermute | solution.py:21
  91.7 8.3 %collective-permute-start.4 = (f32[256,128]{1,0:T(8,128)S(1)}, f32[256,128]{1,0:T(8,128)S(1)}, u32[]{:S(2)}, u32[]{:S(2)}) collective-permute-start(f32[256,128]{1,0:T(8,128)S(1)} %slice_select_fusion), channel_id=1, source_target_pairs={{7,0},{0,1},{1,2},{2,3},{3,4},{4,5},{5,6},{6,7},{15,8},{8,9},{9,10... | collective-permute-start | bytes 393224 | tf_op jit(solution)/shard_map/ppermute | solution.py:21
  96.8 30.3 %collective-permute-start.5 = (f32[2352,128]{1,0:T(8,128)S(1)}, f32[2352,128]{1,0:T(8,128)S(1)}, u32[]{:S(2)}, u32[]{:S(2)}) collective-permute-start(f32[2352,128]{1,0:T(8,128)S(1)} %fusion.16), channel_id=1, source_target_pairs={{7,0},{0,1},{1,2},{2,3},{3,4},{4,5},{5,6},{6,7},{15,8},{8,9},{9,10... | collective-permute-start | bytes 3612680 | tf_op jit(solution)/shard_map/ppermute | solution.py:21

commit v3 on v1

--- a/solution.py
+++ b/solution.py
@@ -210,7 +210,9 @@
         mover = jnp.where(lead_moves, lead, tail)
         stayer = jnp.where(lead_moves, tail, lead)
         mover_behind = from_behind(mover, "pair", 1)
-        moving, behind = lax.optimization_barrier((times(pieces[1], mover), behind))
+        moving, behind, stayer = lax.optimization_barrier(
+            (times(pieces[1], mover), behind, stayer)
+        )
         coming = from_behind(moving, "pair", 1)
         stays = [times(piece, stayer) for piece in pieces]
         corner = contract(stays[0], stays[0]) + contract(stays[1], stays[1])

time: 157 us -> 156 us (level)
  starting transfers between devices: 7.99 us -> 5.91 us
    ppermute x6, starting transfers between devices: 7.99 us -> 5.91 us  [from_behind(): return lax.ppermute(block, axis, route)]
  transfers between devices with their start and end apart: 6 -> 6, of which waited for: 4 -> 6; matrix products, arithmetic and copies ran while one was open for 14% -> 14% of each run, Pallas kernels for 24% -> 25%
where the time goes in v3:
time: 156 us
  Pallas kernels  63.5 us (41%)
  waiting for transfers between devices  54 us (35%)
  matrix products  27.3 us (18%)
  starting transfers between devices  5.91 us (4%)
  local copies, waits for them, and re-layouts  2.56 us (2%)
  between operations  2.15 us (1%)
    pallas_call x3, Pallas kernels, solve(): pl.pallas_call(functools.partial(solve_kernel, n, n_pair, final, counts),...  63.5 us
    ppermute x6, waiting for transfers between devices, from_behind(): return lax.ppermute(block, axis, route)  54 us
    dot_general x9, matrix products, contract(): lax.dot_general(left, right, (((0,), (0,)), ((), ())), precision=precise,...  16.7 us
    dot_general x9, matrix products, times(): jnp.dot(left, right, precision=precise, preferred_element_type=jnp.float32)  10.6 us
    ppermute x6, starting transfers between devices, from_behind(): return lax.ppermute(block, axis, route)  5.91 us
  transfers between devices with their start and end apart: 6, of which 6 were waited for; matrix products, arithmetic and copies ran while one was open for 14% of the time, Pallas kernels for 25%

profile of v3, /device:TPU:0, one launch (start us, length us, event | category | flops | bytes accessed | tf_op | source)
XLA Modules:
  0.0 155.6 jit_solution(12622654056482217436)
XLA Ops:
  0.6 1.4 slice.36
  2.0 3.0 %collective-permute-start = (f32[1232,256]{1,0:T(8,128)S(1)}, f32[1232,256]{1,0:T(8,128)S(1)}, u32[]{:S(2)}, u32[]{:S(2)}) collective-permute-start(f32[1232,256]{1,0:T(8,128)S(1)} %slice.36), channel_id=1, source_target_pairs={{7,0},{0,1},{1,2},{2,3},{3,4},{4,5},{5,6},{6,7},{15,8},{8,9},{9,10... | collective-permute-start | bytes 3784712 | tf_op jit(solution)/shard_map/ppermute | solution.py:21
  5.0 6.2 %fusion.37 = f32[256,256]{1,0:T(8,128)S(1)} fusion(f32[3584,256]{1,0:T(8,128)} %param.2), kind=kOutput, calls=%fused_computation.44 | convolution fusion | flops 1409286144 | bytes 3932160 | tf_op jit(solution)/shard_map/dot_general | solution.py:25
  12.5 19.3 %shard_map.41 = (f32[256,256]{1,0:T(8,128)}, f32[256,256]{1,0:T(8,128)S(1)}) custom-call(f32[128,128]{1,0:T(8,128)S(1)} %slice.40.corner, f32[256,128]{1,0:T(8,128)S(1)} %slice.41.edge), custom_call_target="tpu_custom_call" | custom-call | flops 3523215360 | bytes 41943040 | tf_op jit(solution)/shard_map/pallas_call | solution.py:178
  31.9 1.6 %collective-permute-start.1 = (f32[256,128]{1,0:T(8,128)S(1)}, f32[256,128]{1,0:T(8,128)S(1)}, u32[]{:S(2)}, u32[]{:S(2)}) collective-permute-start(f32[256,128]{1,0:T(8,128)S(1)} %get-tuple-element.25), channel_id=1, source_target_pairs={{7,0},{0,1},{1,2},{2,3},{3,4},{4,5},{5,6},{6,7},{15,8},{8,9},{9,10... | collective-permute-start | bytes 393224 | tf_op jit(solution)/shard_map/ppermute | solution.py:21
  34.1 1.1 convolution_bitcast_fusion
  36.5 1.0 collective-permute-start.2
  37.5 2.9 %collective-permute-done.1 = f32[256,128]{1,0:T(8,128)S(1)} collective-permute-done((f32[256,128]{1,0:T(8,128)S(1)}, f32[256,128]{1,0:T(8,128)S(1)}, u32[]{:S(2)}, u32[]{:S(2)}) %collective-permute-start.1) | collective-permute-done | bytes 131104 | tf_op jit(solution)/shard_map/ppermute | solution.py:21
  41.4 1.1 fusion.12
  42.5 1.2 fusion.39
  44.4 1.2 fusion.35
  45.6 23.1 %collective-permute-done.2 = f32[2352,128]{1,0:T(8,128)S(1)} collective-permute-done((f32[2352,128]{1,0:T(8,128)S(1)}, f32[2352,128]{1,0:T(8,128)S(1)}, u32[]{:S(2)}, u32[]{:S(2)}) %collective-permute-start.2) | collective-permute-done | bytes 1204256 | tf_op jit(solution)/shard_map/ppermute | solution.py:21
  68.7 2.1 %fusion.22.edge = f32[256,128]{1,0:T(8,128)S(1)} fusion(f32[256,128]{1,0:T(8,128)S(1)} %fusion.35, f32[2352,128]{1,0:T(8,128)S(1)} %collective-permute-done.2, f32[2352,128]{1,0:T(8,128)S(1)} %bitcast.33), kind=kOutput, calls=%fused_computation.25 | convolution fusion | flops 463056896 | bytes 2670592 | tf_op jit(solution)/shard_map/dot_general | solution.py:25
  70.8 19.3 %shard_map.42 = (f32[256,256]{1,0:T(8,128)}, f32[256,256]{1,0:T(8,128)S(1)}) custom-call(f32[128,128]{1,0:T(8,128)S(1)} %convolution_add_fusion.1.corner, f32[256,128]{1,0:T(8,128)S(1)} %fusion.22.edge), custom_call_target="tpu_custom_call" | custom-call | flops 3523215360 | bytes 41943040 | tf_op jit(solution)/shard_map/pallas_call | solution.py:178
  90.2 1.1 fusion.16
  91.3 2.8 %collective-permute-done.3 = f32[1232,256]{1,0:T(8,128)S(1)} collective-permute-done((f32[1232,256]{1,0:T(8,128)S(1)}, f32[1232,256]{1,0:T(8,128)S(1)}, u32[]{:S(2)}, u32[]{:S(2)}) %collective-permute-start.3) | collective-permute-done | bytes 1261600 | tf_op jit(solution)/shard_map/ppermute | solution.py:21
  94.2 1.1 fusion.15
  96.0 1.2 fusion.41
  97.9 1.4 collective-permute-done.4
  99.9 1.2 fusion.18
  101.1 23.3 %collective-permute-done.5 = f32[2352,128]{1,0:T(8,128)S(1)} collective-permute-done((f32[2352,128]{1,0:T(8,128)S(1)}, f32[2352,128]{1,0:T(8,128)S(1)}, u32[]{:S(2)}, u32[]{:S(2)}) %collective-permute-start.5) | collective-permute-done | bytes 1204256 | tf_op jit(solution)/shard_map/ppermute | solution.py:21
  124.5 2.2 %fusion.23.edge = f32[256,128]{1,0:T(8,128)S(1)} fusion(f32[256,128]{1,0:T(8,128)S(1)} %fusion.18, f32[2352,128]{1,0:T(8,128)S(1)} %collective-permute-done.5, f32[2352,128]{1,0:T(8,128)S(1)} %fusion.15), kind=kOutput, calls=%fused_computation.26 | convolution fusion | flops 463056896 | bytes 2670592 | tf_op jit(solution)/shard_map/dot_general | solution.py:25
  126.6 24.9 %shard_map.43 = (f32[256,256]{1,0:T(8,128)}, f32[256,256]{1,0:T(8,128)S(1)}, f32[1,256]{1,0:T(1,128)S(1)}) custom-call(f32[128,128]{1,0:T(8,128)S(1)} %convolution_add_fusion.corner, f32[256,128]{1,0:T(8,128)S(1)} %fusion.23.edge), custom_call_target="tpu_custom_call" | custom-call | flops 3523215360 | bytes 41943040 | tf_op jit(solution)/shard_map/pallas_call | solution.py:178
  151.6 3.5 %fusion = f32[3584,256]{1,0:T(8,128)} fusion(f32[256,256]{1,0:T(8,128)S(1)} %get-tuple-element.20, f32[2352,128]{1,0:T(8,128)S(1)} %collective-permute-done.5, f32[2352,128]{1,0:T(8,128)S(1)} %fusion.15, f32[1232,128]{1,0:T(8,128)S(1)} %fusion.40, f32[1232,128]{1,0:T(8,128)S(1)} %fusion.34), kind=kOutput, calls=%fused_computation.1 | convolution fusion | flops 1412038656 | bytes 7602176 | tf_op jit(solution)/shard_map/dot_general | solution.py:31
  (21 shorter events, 6.3 us)
Async XLA Ops:
  2.0 9.2 %copy-start.1 = (s32[2,1]{0,1:T(1,128)S(1)}, s32[2,1]{0,1:T(1,128)}, u32[]{:S(2)}) copy-start(s32[2,1]{0,1:T(1,128)} %param.3) | copy-start | bytes 28
  2.0 33.8 %collective-permute-start = (f32[1232,256]{1,0:T(8,128)S(1)}, f32[1232,256]{1,0:T(8,128)S(1)}, u32[]{:S(2)}, u32[]{:S(2)}) collective-permute-start(f32[1232,256]{1,0:T(8,128)S(1)} %slice.36), channel_id=1, source_target_pairs={{7,0},{0,1},{1,2},{2,3},{3,4},{4,5},{5,6},{6,7},{15,8},{8,9},{9,10... | collective-permute-start | bytes 3784712 | tf_op jit(solution)/shard_map/ppermute | solution.py:21
  12.5 21.6 %copy-start = (f32[3584,256]{1,0:T(8,128)S(1)}, f32[3584,256]{1,0:T(8,128)}, u32[]{:S(2)}) copy-start(f32[3584,256]{1,0:T(8,128)} %param.2) | copy-start | bytes 11010052
  31.9 8.5 %collective-permute-start.1 = (f32[256,128]{1,0:T(8,128)S(1)}, f32[256,128]{1,0:T(8,128)S(1)}, u32[]{:S(2)}, u32[]{:S(2)}) collective-permute-start(f32[256,128]{1,0:T(8,128)S(1)} %get-tuple-element.25), channel_id=1, source_target_pairs={{7,0},{0,1},{1,2},{2,3},{3,4},{4,5},{5,6},{6,7},{15,8},{8,9},{9,10... | collective-permute-start | bytes 393224 | tf_op jit(solution)/shard_map/ppermute | solution.py:21
  36.5 32.2 %collective-permute-start.2 = (f32[2352,128]{1,0:T(8,128)S(1)}, f32[2352,128]{1,0:T(8,128)S(1)}, u32[]{:S(2)}, u32[]{:S(2)}) collective-permute-start(f32[2352,128]{1,0:T(8,128)S(1)} %convolution_bitcast_fusion), channel_id=1, source_target_pairs={{7,0},{0,1},{1,2},{2,3},{3,4},{4,5},{5,6},{6,7},{15,8},{8,9},{9,10... | collective-permute-start | bytes 3612680 | tf_op jit(solution)/shard_map/ppermute | solution.py:21
  41.1 53.0 %collective-permute-start.3 = (f32[1232,256]{1,0:T(8,128)S(1)}, f32[1232,256]{1,0:T(8,128)S(1)}, u32[]{:S(2)}, u32[]{:S(2)}) collective-permute-start(f32[1232,256]{1,0:T(8,128)S(1)} %pad_maximum_fusion.4), channel_id=1, source_target_pairs={{7,0},{0,1},{1,2},{2,3},{3,4},{4,5},{5,6},{6,7},{15,8},{8,9},{9,10... | collective-permute-start | bytes 3784712 | tf_op jit(solution)/shard_map/ppermute | solution.py:21
  90.2 9.1 %collective-permute-start.4 = (f32[256,128]{1,0:T(8,128)S(1)}, f32[256,128]{1,0:T(8,128)S(1)}, u32[]{:S(2)}, u32[]{:S(2)}) collective-permute-start(f32[256,128]{1,0:T(8,128)S(1)} %get-tuple-element.23), channel_id=1, source_target_pairs={{7,0},{0,1},{1,2},{2,3},{3,4},{4,5},{5,6},{6,7},{15,8},{8,9},{9,10... | collective-permute-start | bytes 393224 | tf_op jit(solution)/shard_map/ppermute | solution.py:21
  94.2 30.3 %collective-permute-start.5 = (f32[2352,128]{1,0:T(8,128)S(1)}, f32[2352,128]{1,0:T(8,128)S(1)}, u32[]{:S(2)}, u32[]{:S(2)}) collective-permute-start(f32[2352,128]{1,0:T(8,128)S(1)} %fusion.16), channel_id=1, source_target_pairs={{7,0},{0,1},{1,2},{2,3},{3,4},{4,5},{5,6},{6,7},{15,8},{8,9},{9,10... | collective-permute-start | bytes 3612680 | tf_op jit(solution)/shard_map/ppermute | solution.py:21
